TPU v7x, 512 devices: a whole 4x8x8 slice. The times are simulated.
512 devices in a mesh: dp: 64 (over x, y_lo, z), tensor: 8 (over y_hi, core).
Axes of the slice: x: 4, y: 8 (y_hi: 4, y_lo: 2; y = y_hi * 2 + y_lo), z: 8, core: 2. Of those that a mesh axis runs over, the one named last changes fastest.
Arguments:
- tokens: bfloat16 [32768, 1024], P('dp', 'tensor'), may hold values from -6 to 6
- cotangent: bfloat16 [32768, 1024], P('dp', 'tensor'), may hold values from -6 to 6
- w_in: bfloat16 [4096, 1024], P(('dp', 'tensor')), may hold values from -0.1875 to 0.1875
- b_in: bfloat16 [4096], P(('dp', 'tensor')), may hold values from -4 to 4
- w_out: bfloat16 [4096, 1024], P(('dp', 'tensor')), may hold values from -0.09375 to 0.09375
Outputs:
- mixed: bfloat16 [32768, 1024], P('dp', 'tensor')
- grad_in: float32 [4096, 1024], P(('dp', 'tensor'))
All inputs are finite; a program needn't handle non-finite values.
Results may differ from a plain program's by a relative error of at most 0.017.
Values may be sent and summed in bfloat16 or wider, within the bound.
A program may use at most 64 MiB of HBM per device.

v0:
```python
import math

import jax
import jax.numpy as jnp
from jax import lax
from jax.sharding import PartitionSpec as P


def gelu_parts(value):
    coeff = 0.7978845608
    inner = coeff * (value + 0.044715 * value * value * value)
    tangent = jnp.tanh(inner)
    result = 0.5 * value * (1.0 + tangent)
    slope = 0.5 * (1.0 + tangent) + 0.5 * value * (1.0 - tangent * tangent) * coeff * (
        1.0 + 3.0 * 0.044715 * value * value
    )
    return (result, slope)


def on_device(tokens, cotangent, w_in, b_in, w_out):
    contract_last = (((1,), (1,)), ((), ()))
    contract_first = (((0,), (0,)), ((), ()))
    total_rows = tokens.shape[0] * lax.axis_size("dp")
    scale = 1.0 / math.sqrt(total_rows)
    tok_full, cot_full = (
        lax.all_gather(tokens, "tensor", axis=1, tiled=True),
        lax.all_gather(cotangent, "tensor", axis=1, tiled=True),
    )
    in_rows, bias_rows = (
        lax.all_gather(w_in, "dp", axis=0, tiled=True),
        lax.all_gather(b_in, "dp", axis=0, tiled=True),
    )
    proj_rows = lax.all_gather(w_out, "dp", axis=0, tiled=True)
    pre = lax.dot_general(
        tok_full, in_rows, contract_last, preferred_element_type=jnp.float32
    ) + bias_rows.astype(jnp.float32)
    act_value, slope = gelu_parts(pre)
    act = act_value.astype(jnp.bfloat16)
    term = jnp.dot(act, proj_rows, preferred_element_type=jnp.float32)
    mixed = lax.psum_scatter(term.astype(jnp.bfloat16), "tensor", scatter_dimension=1, tiled=True)
    dact = lax.dot_general(cot_full, proj_rows, contract_last, preferred_element_type=jnp.float32)
    dpre = (dact * slope).astype(jnp.bfloat16)
    grad_sum = lax.psum_scatter(
        lax.dot_general(dpre, tok_full, contract_first, preferred_element_type=jnp.float32),
        "dp",
        scatter_dimension=0,
        tiled=True,
    )
    grad_in = grad_sum * scale
    return (mixed, grad_in)


def solution(mesh):
    in_specs = (
        P("dp", "tensor"),
        P("dp", "tensor"),
        P(("dp", "tensor"), None),
        P(("dp", "tensor")),
        P(("dp", "tensor"), None),
    )
    out_specs = (P("dp", "tensor"), P(("dp", "tensor"), None))
    return jax.shard_map(
        on_device, mesh=mesh, in_specs=in_specs, out_specs=out_specs, check_vma=False
    )
```

profile of v0, /device:TPU:16, one launch (start us, length us, event | category | flops | bytes accessed | tf_op | source)
XLA Modules:
  0.0 1057.3 jit_solution(10773823409074904943)
XLA Ops:
  7.2 0.0 all-gather.5.cloned.1.call-start
  7.2 0.7 all-gather.5.cloned.1.call-update
  7.9 0.0 all-gather.7.cloned.1.call-start
  7.9 0.7 all-gather.7.cloned.1.call-update
  8.6 0.0 all-gather.9.cloned.1.call-start
  8.7 0.7 all-gather.9.cloned.1.call-update
  9.4 0.0 all-gather.11.cloned.1.call-start
  9.4 0.5 all-gather.11.cloned.1.call-update
  10.0 0.0 reduce-scatter.7.cloned.1.call-start
  10.0 1.3 dynamic-slice
  11.9 0.9 dynamic-update-slice
  12.8 165.2 %all-reduce = bf16[512]{0:T(512)(128)(2,1)S(1)} all-reduce(bf16[512]{0:T(512)(128)(2,1)S(1)} %dynamic-update-slice), channel_id=1, replica_groups=mesh['dp'=64,'tensor'=8] {'dp'}, use_global_device_ids=true, to_apply=%add | all-reduce | flops 512 | bytes 2048
  178.0 0.0 all-gather.5.cloned.1.call-done
  178.1 172.9 %all-gather.7.cloned.1.call-done = bf16[512,1024]{1,0:T(8,128)(2,1)} async-done(((bf16[8,1024]{1,0:T(8,128)(2,1)}), bf16[512,1024]{1,0:T(8,128)(2,1)}) %all-gather.7.cloned.1.call-update) | async-done | bytes 1048592 | tf_op jit(solution)/shard_map/all_gather | solution.py:30
  350.9 2.3 convolution_add_fusion
  353.2 0.0 copy-start.2
  353.2 296.4 %all-gather.9.cloned.1.call-done = bf16[512,1024]{1,0:T(8,128)(2,1)} async-done(((bf16[8,1024]{1,0:T(8,128)(2,1)}), bf16[512,1024]{1,0:T(8,128)(2,1)}) %all-gather.9.cloned.1.call-update) | async-done | bytes 1048592 | tf_op jit(solution)/shard_map/all_gather | solution.py:33
  649.6 0.0 copy-done.2
  649.6 2.0 convolution_convert_fusion
  651.6 0.0 copy-start
  651.6 0.0 copy-start.1
  651.7 1.3 copy.7
  653.0 0.0 reduce-scatter.7.cloned.1.call-update
  653.0 0.0 reduce-scatter.5.cloned.1.call-start
  653.1 28.7 %all-gather.11.cloned.1.call-done = bf16[512,1024]{1,0:T(8,128)(2,1)} async-done(((bf16[512,128]{1,0:T(8,128)(2,1)}), bf16[512,1024]{1,0:T(8,128)(2,1)}) %all-gather.11.cloned.1.call-update) | async-done | bytes 1048592 | tf_op jit(solution)/shard_map/all_gather | solution.py:27
  681.8 0.0 copy-done
  681.8 4.7 fusion.1
  686.4 0.0 reduce-scatter.5.cloned.1.call-update
  686.5 35.6 %reduce-scatter.7.cloned.1.call-done = bf16[128,512]{1,0:T(8,128)(2,1)} async-done(((bf16[1024,512]{1,0:T(8,128)(2,1)}), bf16[128,512]{1,0:T(8,128)(2,1)}) %reduce-scatter.7.cloned.1.call-update) | async-done | bytes 131088
  722.1 1.7 copy.8
  723.7 325.3 %reduce-scatter.5.cloned.1.call-done = f32[8,1024]{1,0:T(8,128)} async-done(((f32[512,1024]{1,0:T(8,128)}), f32[8,1024]{1,0:T(8,128)}) %reduce-scatter.5.cloned.1.call-update) | async-done | bytes 32784 | tf_op jit(solution)/shard_map/reduce_scatter | solution.py:43
  1049.1 1.4 broadcast_multiply_fusion
  (3 shorter events, 0.0 us)
Async XLA Ops:
  7.2 170.9 %all-gather.5.cloned.1.call-start = ((), (), s32[]{:S(2)}) async-start(), calls=%async_computation.2 | async-start | bytes 1179648 | tf_op jit(solution)/shard_map/all_gather | solution.py:26
  7.9 343.0 %all-gather.7.cloned.1.call-start = ((), (), s32[]{:S(2)}) async-start(), calls=%async_computation.3 | async-start | bytes 1064960 | tf_op jit(solution)/shard_map/all_gather | solution.py:30
  8.6 640.9 %all-gather.9.cloned.1.call-start = ((), (), s32[]{:S(2)}) async-start(), calls=%async_computation.4 | async-start | bytes 1064960 | tf_op jit(solution)/shard_map/all_gather | solution.py:33
  9.4 672.4 %all-gather.11.cloned.1.call-start = ((), (), s32[]{:S(2)}) async-start(), calls=%async_computation.5 | async-start | bytes 1179648 | tf_op jit(solution)/shard_map/all_gather | solution.py:27
  10.0 712.1 %reduce-scatter.7.cloned.1.call-start = ((), (), s32[]{:S(2)}) async-start(), calls=%async_computation.7 | async-start | bytes 1179648
  353.2 296.4 %copy-start.2 = (f32[512,512]{1,0:T(8,128)}, f32[512,512]{1,0:T(8,128)S(1)}, u32[]{:S(2)}) copy-start(f32[512,512]{1,0:T(8,128)S(1)} %convolution_add_fusion) | copy-start | bytes 3145732
  651.6 30.1 %copy-start = (bf16[512,1024]{1,0:T(8,128)(2,1)S(1)}, bf16[512,1024]{1,0:T(8,128)(2,1)}, u32[]{:S(2)}) copy-start(bf16[512,1024]{1,0:T(8,128)(2,1)} %all-gather.5.cloned.1.call-done) | copy-start | bytes 3145732
  651.6 30.1 %copy-start.1 = (bf16[512,1024]{1,0:T(8,128)(2,1)S(1)}, bf16[512,1024]{1,0:T(8,128)(2,1)}, u32[]{:S(2)}) copy-start(bf16[512,1024]{1,0:T(8,128)(2,1)} %all-gather.9.cloned.1.call-done) | copy-start | bytes 3145732
  653.0 396.1 %reduce-scatter.5.cloned.1.call-start = ((), (), s32[]{:S(2)}) async-start(), calls=%async_computation.6 | async-start | bytes 2129920 | tf_op jit(solution)/shard_map/reduce_scatter | solution.py:43
Sparse Core Ops, SparseCore 0:
  10.1 38.2 all-gather.4
  50.5 300.3 all-gather.6
  353.0 296.5 all-gather.8
  651.6 30.1 all-gather.10
  684.4 37.6 reduce-scatter.6
  724.7 324.3 reduce-scatter.4
where the time goes:
time: 1060 us
  waiting for transfers between devices  862 us (81%)
  blocking collectives  165 us (16%)
  between operations  14.8 us (1%)
    reduce_scatter x1, waiting for transfers between devices, on_device(): lax.psum_scatter(lax.dot_general(dpre, tok_full, contract_first, preferre...  325 us
    all_gather x1, waiting for transfers between devices, on_device(): proj_rows = lax.all_gather(w_out, 'dp', axis=0, tiled=True)  296 us
    all_gather x1, waiting for transfers between devices, on_device(): lax.all_gather(w_in, 'dp', axis=0, tiled=True)  173 us
    unnamed x1, blocking collectives  165 us
    unnamed x7, waiting for transfers between devices  38.2 us
    all_gather x1, waiting for transfers between devices, on_device(): lax.all_gather(cotangent, 'tensor', axis=1, tiled=True)  28.7 us
  transfers between devices with their start and end apart: 6, of which 5 were waited for; matrix products, arithmetic and copies ran while one was open for 1% of the time, Pallas kernels for 0%

commit v1 on v0

v1 whole, which is shorter than its diff:
```python
import math

import jax
import jax.numpy as jnp
from jax import lax
from jax.experimental import pallas as pl
from jax.experimental.pallas import tpu as pltpu
from jax.sharding import PartitionSpec as P

MESH = pl.DeviceIdType.MESH
BF16, F32 = jnp.bfloat16, jnp.float32
NX, NL, NZ, NY = 4, 2, 8, 4
ROWS, D, OWN = 512, 1024, 8
UNITS = NX * NL * NZ * OWN
BW = D + 128
HALF = ROWS // 2


def gelu_parts(value):
    coeff = 0.7978845608
    square = value * value
    tangent = jnp.tanh(coeff * value * (1.0 + 0.044715 * square))
    half = 0.5 * (1.0 + tangent)
    slope = half + 0.5 * value * (1.0 - tangent * tangent) * coeff * (1.0 + 3.0 * 0.044715 * square)
    return value * half, slope


def kernel(
    tok_in, cot_in, win_in, b_in, wout_in, mixed_out, grad_out,
    tok, cot, w_i, w_o, act, slope, dpre, mix_s, mix_r, mix_o, mix_in, g_s, g_r, g_p, g_q,
    send_sem, recv_sem,
):
    d, t = lax.axis_index("dp"), lax.axis_index("tensor")
    x, yl, z = d // (NL * NZ), (d // NZ) % NL, d % NZ
    yh, c = t // 2, t % 2

    def peer(dx=0, dl=0, dz=0, dy=0, dc=0):
        px, pz, py = (x + dx + NX) % NX, (z + dz + NZ) % NZ, (yh + dy + NY) % NY
        return ((px * NL + (yl + dl) % NL) * NZ + pz, py * 2 + (c + dc) % 2)

    count = [0]
    started = []

    def send(src, dst, to):
        k = count[0]
        count[0] += 1
        copy = pltpu.make_async_remote_copy(
            src_ref=src, dst_ref=dst, send_sem=send_sem.at[k], recv_sem=recv_sem.at[k],
            device_id=to, device_id_type=MESH,
        )
        copy.start()
        started.append(copy)
        return copy

    near_x = [dict(dx=i) for i in (2, 1, -1)]
    near_lz = [dict(dz=i, dl=l) for i in (4, 3, -3, 2, -2, 1, -1, 0) for l in (1, 0) if (i, l) != (0, 0)]
    near_xl = [dict(dx=i, dl=l) for i in (2, 1, -1, 0) for l in (1, 0) if (i, l) != (0, 0)]
    near_y = [dict(dy=i) for i in (2, 1, -1)]
    sibling = dict(dc=1)

    barrier = pltpu.get_barrier_semaphore()
    greeted = near_lz + near_x + [p for p in near_xl if p.get("dl") and p.get("dx")] + near_y + [sibling]
    for p in greeted:
        pl.semaphore_signal(barrier, inc=1, device_id=peer(**p), device_id_type=MESH)

    own_columns = pl.ds(pl.multiple_of(t * 128, 128), 128)
    tok[:, own_columns] = tok_in[...]
    cot[:, own_columns] = cot_in[...]
    eye = lax.broadcasted_iota(jnp.int32, (OWN, OWN), 0) == lax.broadcasted_iota(jnp.int32, (OWN, OWN), 1)
    bias = jnp.broadcast_to(b_in[...].astype(F32), (OWN, OWN))
    bias = jnp.sum(jnp.where(eye, bias, 0.0), axis=1, keepdims=True)
    w_i[x, yl, z, :, 0:D] = win_in[...]
    w_i[x, yl, z, :, D:BW] = jnp.broadcast_to(bias, (OWN, 128)).astype(BF16)
    w_o[x, yl, z] = wout_in[...]
    pl.semaphore_wait(barrier, len(greeted))

    def columns(dy, dc=0):
        py, pc = (yh + dy + NY) % NY, (c + dc) % 2
        return pl.ds(pl.multiple_of(py * 256 + pc * 128, 128), 128)

    top, bottom, whole = pl.ds(0, HALF), pl.ds(HALF, HALF), pl.ds(0, ROWS)

    def place(buf, rows, dy):
        return buf.at[rows, columns(dy)]

    def spread(buf):
        out = {}
        out["up_a"] = send(place(buf, top, 0), place(buf, top, 0), peer(dy=1))
        out["dn_b"] = send(place(buf, bottom, 0), place(buf, bottom, 0), peer(dy=-1))
        out["up_b"] = send(place(buf, bottom, 0), place(buf, bottom, 0), peer(dy=1))
        out["dn_a"] = send(place(buf, top, 0), place(buf, top, 0), peer(dy=-1))
        out["sib"] = [send(place(buf, whole, 0), place(buf, whole, 0), peer(**sibling))]
        return out

    def pass_on(buf, out):
        out["up_a"].wait_recv()
        out["fw_a"] = send(place(buf, top, -1), place(buf, top, -1), peer(dy=1))
        out["dn_b"].wait_recv()
        out["fw_b"] = send(place(buf, bottom, 1), place(buf, bottom, 1), peer(dy=-1))

    def share(buf, out, near):
        if near:
            for key, dy in (("up_b", -1), ("dn_a", 1)):
                out[key].wait_recv()
                out["sib"].append(send(place(buf, whole, dy), place(buf, whole, dy), peer(**sibling)))
        else:
            for key, rows in (("fw_a", top), ("fw_b", bottom)):
                out[key].wait_recv()
                out["sib"].append(send(place(buf, rows, 2), place(buf, rows, 2), peer(**sibling)))

    def settle(out):
        for copy in out["sib"]:
            copy.wait_recv()

    tok_moves = spread(tok)
    wo_first = [send(w_o.at[x, yl, z], w_o.at[x, yl, z], peer(**p)) for p in near_xl]
    wi_first = [send(w_i.at[x, yl, z], w_i.at[x, yl, z], peer(**p)) for p in near_lz]

    def ring_step(step):
        back, ahead = (z - step + 1 + NZ) % NZ, (z + step - 1) % NZ
        xs_up, xs_dn = pl.ds(0, NX), pl.ds(0, NX)
        if step == NZ // 2:
            xs_up, xs_dn = pl.ds(0, NX // 2), pl.ds(NX // 2, NX // 2)
        return [
            send(w_o.at[xs_up, :, back], w_o.at[xs_up, :, back], peer(dz=1)),
            send(w_o.at[xs_dn, :, ahead], w_o.at[xs_dn, :, ahead], peer(dz=-1)),
        ]

    def arrive(moves):
        for copy in moves:
            copy.wait_recv()

    arrive(wo_first)
    ring = ring_step(1)
    pass_on(tok, tok_moves)
    cot_moves = spread(cot)
    arrive(wi_first)
    wi_second = [send(w_i.at[x], w_i.at[x], peer(**p)) for p in near_x]
    share(tok, tok_moves, True)
    arrive(ring)
    ring = ring_step(2)
    share(tok, tok_moves, False)
    pass_on(cot, cot_moves)
    arrive(ring)
    ring = ring_step(3)
    arrive(wi_second)
    settle(tok_moves)

    def part(ref, j, width):
        value = ref[2 * j : 2 * j + 2].astype(F32)
        return value.reshape(UNITS // 2, width).astype(BF16)

    last = (((1,), (1,)), ((), ()))
    first = (((0,), (0,)), ((), ()))
    pick = (lax.broadcasted_iota(jnp.int32, (OWN, 128), 1) == 0).astype(F32).astype(BF16)
    for j in range(2):
        rows = part(w_i, j, BW)
        bias = lax.dot_general(pick, rows[:, D:BW], last, preferred_element_type=F32)
        pre = lax.dot_general(tok[...], rows[:, 0:D], last, preferred_element_type=F32) + bias[0:1, :]
        value, grade = gelu_parts(pre)
        act[:, j * 256 : (j + 1) * 256] = value.astype(BF16)
        slope[:, j * 256 : (j + 1) * 256] = grade
        if j == 0:
            arrive(ring)
            ring = ring_step(4)
            share(cot, cot_moves, True)
    arrive(ring)

    pair = []
    for k, dy in enumerate((2, 1, -1, 0)):
        span = pl.ds(pl.multiple_of(((yh + dy + NY) % NY) * 256, 256), 256)
        weights = w_o[:, :, :, :, span].astype(F32).reshape(UNITS, 256).astype(BF16)
        term = jnp.dot(act[...], weights, preferred_element_type=F32)
        mix_s[k] = term.astype(BF16)
        theirs = pl.ds(pl.multiple_of((1 - c) * 128, 128), 128)
        pair.append(send(mix_s.at[k, :, theirs], mix_r.at[k], peer(**sibling)))
    share(cot, cot_moves, False)
    mine = pl.ds(pl.multiple_of(c * 128, 128), 128)
    out_moves = []
    for k, p in enumerate(near_y):
        pair[k].wait_recv()
        mix_o[k] = (mix_s[k, :, mine].astype(F32) + mix_r[k].astype(F32)).astype(BF16)
        out_moves.append(send(mix_o.at[k], mix_in.at[k], peer(**p)))
    settle(cot_moves)

    for j in range(2):
        dact = lax.dot_general(cot[...], part(w_o, j, D), last, preferred_element_type=F32)
        cols = slice(j * 256, (j + 1) * 256)
        dpre[:, cols] = (dact * slope[:, cols]).astype(BF16)

    def grads(px):
        units = pl.ds(pl.multiple_of(px * 128, 128), 128)
        return lax.dot_general(dpre[:, units], tok[...], first, preferred_element_type=F32).reshape(NL, NZ, OWN, D)

    x_moves = []
    for k, p in enumerate(near_x):
        g_s[k] = grads((x + p["dx"] + NX) % NX).astype(BF16)
        x_moves.append(send(g_s.at[k], g_r.at[k], peer(**p)))
    total = grads(x)

    pair[3].wait_recv()
    result = mix_s[3, :, mine].astype(F32) + mix_r[3].astype(F32)
    for k in range(3):
        out_moves[k].wait_recv()
        result = result + mix_in[k].astype(F32)
    mixed_out[...] = result.astype(BF16)

    arrive(x_moves)
    total = total + (g_r[0].astype(F32) + g_r[1].astype(F32) + g_r[2].astype(F32))
    g_p[...] = total.astype(BF16)
    lz_moves = []
    for k, p in enumerate(near_lz):
        block = g_p.at[(yl + p["dl"]) % NL, (z + p["dz"] + NZ) % NZ]
        lz_moves.append(send(block, g_q.at[k], peer(**p)))
    total = g_p[yl, z].astype(F32)
    for k in range(len(near_lz)):
        lz_moves[k].wait_recv()
        total = total + g_q[k].astype(F32)
    grad_out[...] = total * (1.0 / math.sqrt(ROWS * NX * NL * NZ))

    for copy in started:
        copy.wait_send()


def on_device(tokens, cotangent, w_in, b_in, w_out):
    vmem = pl.BlockSpec(memory_space=pltpu.VMEM)
    return pl.pallas_call(
        kernel,
        out_shape=(
            jax.ShapeDtypeStruct((ROWS, 128), BF16),
            jax.ShapeDtypeStruct((OWN, D), F32),
        ),
        in_specs=[vmem] * 5,
        out_specs=(vmem, vmem),
        scratch_shapes=[
            pltpu.VMEM((ROWS, D), BF16),
            pltpu.VMEM((ROWS, D), BF16),
            pltpu.VMEM((NX, NL, NZ, OWN, BW), BF16),
            pltpu.VMEM((NX, NL, NZ, OWN, D), BF16),
            pltpu.VMEM((ROWS, UNITS), BF16),
            pltpu.VMEM((ROWS, UNITS), F32),
            pltpu.VMEM((ROWS, UNITS), BF16),
            pltpu.VMEM((4, ROWS, 256), BF16),
            pltpu.VMEM((4, ROWS, 128), BF16),
            pltpu.VMEM((3, ROWS, 128), BF16),
            pltpu.VMEM((3, ROWS, 128), BF16),
            pltpu.VMEM((3, NL, NZ, OWN, D), BF16),
            pltpu.VMEM((3, NL, NZ, OWN, D), BF16),
            pltpu.VMEM((NL, NZ, OWN, D), BF16),
            pltpu.VMEM((NL * NZ - 1, OWN, D), BF16),
            pltpu.SemaphoreType.DMA((90,)),
            pltpu.SemaphoreType.DMA((90,)),
        ],
        compiler_params=pltpu.CompilerParams(
            collective_id=0, has_side_effects=True, vmem_limit_bytes=48 * 1024 * 1024
        ),
        cost_estimate=pl.CostEstimate(flops=2147483648, bytes_accessed=8388608, transcendentals=262144),
    )(tokens, cotangent, w_in, b_in.reshape(1, OWN), w_out)


def solution(mesh):
    in_specs = (
        P("dp", "tensor"),
        P("dp", "tensor"),
        P(("dp", "tensor"), None),
        P(("dp", "tensor")),
        P(("dp", "tensor"), None),
    )
    out_specs = (P("dp", "tensor"), P(("dp", "tensor"), None))
    return jax.shard_map(
        on_device, mesh=mesh, in_specs=in_specs, out_specs=out_specs, check_vma=False
    )
```

time: 1060 us -> 83.6 us (0.08)
  the two profiles are of different devices: /device:TPU:16 before, /device:TPU:1 now
where the time goes in v1:
time: 83.6 us; the launch traced here: 83.3 us
  Pallas kernels  77.5 us (93%)
  local copies, waits for them, and re-layouts  5.16 us (6%)
    pallas_call x1, Pallas kernels, on_device(): pl.pallas_call(kernel, out_shape=(jax.ShapeDtypeStruct((ROWS, 128), BF16)...  77.5 us
    unnamed x12, local copies, waits for them, and re-layouts  5.16 us

profile of v1, /device:TPU:1, one launch (start us, length us, event | category | flops | bytes accessed | tf_op | source)
XLA Modules:
  0.0 83.3 jit_solution(5323890488065297628)
XLA Ops:
  0.6 0.0 copy-start.4
  0.6 0.6 copy-done.4
  1.3 0.0 copy-start
  1.3 0.9 %copy-done = bf16[512,128]{1,0:T(8,128)(2,1)S(1)} copy-done((bf16[512,128]{1,0:T(8,128)(2,1)S(1)}, bf16[512,128]{1,0:T(8,128)(2,1)}, u32[]{:S(2)}) %copy-start) | copy-done | bytes 131096
  2.2 0.0 copy-start.1
  2.2 0.9 %copy-done.1 = bf16[512,128]{1,0:T(8,128)(2,1)S(1)} copy-done((bf16[512,128]{1,0:T(8,128)(2,1)S(1)}, bf16[512,128]{1,0:T(8,128)(2,1)}, u32[]{:S(2)}) %copy-start.1) | copy-done | bytes 131096
  3.1 0.0 copy-start.2
  3.1 0.7 copy-done.2
  3.8 0.0 copy-start.3
  3.8 0.7 copy-done.3
  4.5 77.5 %shard_map.68 = (bf16[512,128]{1,0:T(8,128)(2,1)S(1)}, f32[8,1024]{1,0:T(8,128)S(1)}) custom-call(bf16[512,128]{1,0:T(8,128)(2,1)S(1)} %copy-done, bf16[512,128]{1,0:T(8,128)(2,1)S(1)} %copy-done.1, bf16[8,1024]{1,0:T(8,128)(2,1)S(1)} %copy-done.2, bf16[1,8]{1,0:T(2,128)(2,1)S(1)} %bitcast.1, bf16[8,1024]{1,0:T(8,128)(2,1)S(1)} %copy-done.3), custom_call_target="tpu_custom_call" | custom-call | flops 2147483648 | bytes 8388608 | tf_op jit(solution)/shard_map/pallas_call | solution.py:227
  82.0 0.7 copy.9
  82.7 0.6 copy.10
Async XLA Ops:
  0.6 0.7 copy-start.4
  1.3 0.9 %copy-start = (bf16[512,128]{1,0:T(8,128)(2,1)S(1)}, bf16[512,128]{1,0:T(8,128)(2,1)}, u32[]{:S(2)}) copy-start(bf16[512,128]{1,0:T(8,128)(2,1)} %tok_in.1) | copy-start | bytes 393220
  2.2 0.9 %copy-start.1 = (bf16[512,128]{1,0:T(8,128)(2,1)S(1)}, bf16[512,128]{1,0:T(8,128)(2,1)}, u32[]{:S(2)}) copy-start(bf16[512,128]{1,0:T(8,128)(2,1)} %cot_in.1) | copy-start | bytes 393220
  3.1 0.7 copy-start.2
  3.8 0.7 copy-start.3

commit v2 on v1

v2 whole, which is shorter than its diff:
```python
import math

import jax
import jax.numpy as jnp
from jax import lax
from jax.experimental import pallas as pl
from jax.experimental.pallas import tpu as pltpu
from jax.sharding import PartitionSpec as P

MESH = pl.DeviceIdType.MESH
BF16, F32 = jnp.bfloat16, jnp.float32
NX, NL, NZ, NY = 4, 2, 8, 4
ROWS, D, OWN = 512, 1024, 8
UNITS = NX * NL * NZ * OWN
BW = D + 128
HALF = ROWS // 2
CX = 768


def gelu_parts(value):
    coeff = 0.7978845608
    square = value * value
    tangent = jnp.tanh(coeff * value * (1.0 + 0.044715 * square))
    half = 0.5 * (1.0 + tangent)
    slope = half + 0.5 * value * (1.0 - tangent * tangent) * coeff * (1.0 + 3.0 * 0.044715 * square)
    return value * half, slope


def kernel(
    tok_in, cot_in, win_in, b_in, wout_in, mixed_out, grad_out,
    tok, cot, w_i, w_o, b_own, act, slope, dpre, mix_s, mix_r, mix_o, mix_in,
    g_s, g_r, g_p, g_q, h_s, h_r, h_p, h_q,
    send_sem, recv_sem, local_sem,
):
    d, t = lax.axis_index("dp"), lax.axis_index("tensor")
    x, yl, z = d // (NL * NZ), (d // NZ) % NL, d % NZ
    yh, c = t // 2, t % 2

    def peer(dx=0, dl=0, dz=0, dy=0, dc=0):
        px, pz, py = (x + dx + NX) % NX, (z + dz + NZ) % NZ, (yh + dy + NY) % NY
        return ((px * NL + (yl + dl) % NL) * NZ + pz, py * 2 + (c + dc) % 2)

    count = [0]
    started = []

    def send(src, dst, to):
        k = count[0]
        count[0] += 1
        copy = pltpu.make_async_remote_copy(
            src_ref=src, dst_ref=dst, send_sem=send_sem.at[k], recv_sem=recv_sem.at[k],
            device_id=to, device_id_type=MESH,
        )
        copy.start()
        started.append(copy)
        return copy

    near_x = [dict(dx=i) for i in (2, 1, -1)]
    near_z = [dict(dz=i) for i in (1, -1, 2, -2, 3, -3, 4)]
    near_xl = [dict(dx=i, dl=l) for i in (2, 1, -1, 0) for l in (1, 0) if (i, l) != (0, 0)]
    near_lz = [dict(dz=i, dl=l) for i in (4, 3, -3, 2, -2, 1, -1, 0) for l in (1, 0) if (i, l) != (0, 0)]
    near_y = [dict(dy=i) for i in (2, 1, -1)]
    sibling, partner = dict(dc=1), dict(dl=1)

    barrier = pltpu.get_barrier_semaphore()
    greeted = near_lz + [p for p in near_xl if p["dx"]] + near_y + [sibling]
    for p in greeted:
        pl.semaphore_signal(barrier, inc=1, device_id=peer(**p), device_id_type=MESH)

    own_columns = pl.ds(pl.multiple_of(t * 128, 128), 128)
    local = [
        pltpu.make_async_copy(src, dst, local_sem.at[k])
        for k, (src, dst) in enumerate((
            (b_in, b_own),
            (win_in, w_i.at[x, z, yl, :, pl.ds(0, D)]),
            (wout_in, w_o.at[z, yl, x]),
            (tok_in, tok.at[:, own_columns]),
            (cot_in, cot.at[:, own_columns]),
        ))
    ]
    for copy in local:
        copy.start()
    local[0].wait()
    eye = lax.broadcasted_iota(jnp.int32, (OWN, OWN), 0) == lax.broadcasted_iota(jnp.int32, (OWN, OWN), 1)
    bias = jnp.broadcast_to(b_own[...].astype(F32), (OWN, OWN))
    bias = jnp.sum(jnp.where(eye, bias, 0.0), axis=1, keepdims=True)
    w_i[x, z, yl, :, D:BW] = jnp.broadcast_to(bias, (OWN, 128)).astype(BF16)
    for copy in local[1:]:
        copy.wait()
    pl.semaphore_wait(barrier, len(greeted))

    def columns(dy, dc=0):
        py, pc = (yh + dy + NY) % NY, (c + dc) % 2
        return pl.ds(pl.multiple_of(py * 256 + pc * 128, 128), 128)

    top, bottom, whole = pl.ds(0, HALF), pl.ds(HALF, HALF), pl.ds(0, ROWS)

    def place(buf, rows, dy):
        return buf.at[rows, columns(dy)]

    def spread(buf):
        out = {}
        out["up_a"] = send(place(buf, top, 0), place(buf, top, 0), peer(dy=1))
        out["dn_b"] = send(place(buf, bottom, 0), place(buf, bottom, 0), peer(dy=-1))
        out["up_b"] = send(place(buf, bottom, 0), place(buf, bottom, 0), peer(dy=1))
        out["dn_a"] = send(place(buf, top, 0), place(buf, top, 0), peer(dy=-1))
        out["sib"] = [send(place(buf, whole, 0), place(buf, whole, 0), peer(**sibling))]
        return out

    def pass_on(buf, out):
        out["up_a"].wait_recv()
        out["fw_a"] = send(place(buf, top, -1), place(buf, top, -1), peer(dy=1))
        out["dn_b"].wait_recv()
        out["fw_b"] = send(place(buf, bottom, 1), place(buf, bottom, 1), peer(dy=-1))

    def share(buf, out, near):
        if near:
            for key, dy in (("up_b", -1), ("dn_a", 1)):
                out[key].wait_recv()
                out["sib"].append(send(place(buf, whole, dy), place(buf, whole, dy), peer(**sibling)))
        else:
            for key, rows in (("fw_a", top), ("fw_b", bottom)):
                out[key].wait_recv()
                out["sib"].append(send(place(buf, rows, 2), place(buf, rows, 2), peer(**sibling)))

    def settle(out):
        for copy in out["sib"]:
            copy.wait_recv()

    def arrive(moves):
        for copy in moves:
            copy.wait_recv()

    def wi_to_z(l):
        return [send(w_i.at[x, z, l], w_i.at[x, z, l], peer(**p)) for p in near_z]

    def wi_to_x(dz):
        pz = (z + dz + NZ) % NZ
        return [send(w_i.at[x, pz], w_i.at[x, pz], peer(**p)) for p in near_x]

    def wo_to_x(l):
        return [send(w_o.at[z, l, x], w_o.at[z, l, x], peer(**p)) for p in near_x]

    def ring_step(step, half, before=None):
        l = (yl + half) % NL
        out = []
        for k, sign in enumerate((1, -1)):
            if before is not None:
                before[k].wait_recv()
            if step < NZ // 2 or k == half:
                pz = (z - sign * (step - 1) + NZ) % NZ
                out.append(send(w_o.at[pz, l], w_o.at[pz, l], peer(dz=sign)))
        return out

    tok_moves = spread(tok)
    wi_own = send(w_i.at[x, z, yl], w_i.at[x, z, yl], peer(**partner))
    wo_own = send(w_o.at[z, yl, x], w_o.at[z, yl, x], peer(**partner))
    wo_moves = wo_to_x(yl)
    wi_moves = wi_to_z(yl)
    wi_own.wait_recv()
    wi_more = wi_to_z(1 - yl)
    wi_second = wi_to_x(0)
    wo_own.wait_recv()
    wo_more = wo_to_x(1 - yl)

    def relay(*dzs):
        out = []
        for dz in dzs:
            k = [p["dz"] for p in near_z].index(-dz if dz != 4 else 4)
            wi_moves[k].wait_recv()
            wi_more[k].wait_recv()
            out += wi_to_x(dz)
        return out

    arrive(wo_moves)
    ring = [ring_step(1, 0)]
    wi_second += relay(1, -1)
    arrive(wo_more)
    ring.append(ring_step(1, 1))
    pass_on(tok, tok_moves)
    cot_moves = spread(cot)
    wi_second += relay(2, -2)
    ring = [ring_step(2, h, ring[h]) for h in (0, 1)]
    wi_second += relay(3, -3, 4)
    share(tok, tok_moves, True)
    ring = [ring_step(3, h, ring[h]) for h in (0, 1)]
    share(tok, tok_moves, False)
    pass_on(cot, cot_moves)
    ring = [ring_step(4, h, ring[h]) for h in (0, 1)]
    arrive(wi_second)
    settle(tok_moves)

    last = (((1,), (1,)), ((), ()))

    def rows_of(value):
        return value.astype(F32).reshape(-1, value.shape[-1]).astype(BF16)

    for j in range(2):
        rows = rows_of(w_i[2 * j : 2 * j + 2])
        bias = rows[:, D:BW].astype(F32)
        pre = lax.dot_general(rows[:, 0:D], tok[...], last, preferred_element_type=F32)
        pre = pre + jnp.concatenate([bias] * (ROWS // 128), axis=1)
        value, grade = gelu_parts(pre)
        act[:, j * 256 : (j + 1) * 256] = value.astype(BF16).T
        slope[2 * j] = grade[0:128]
        slope[2 * j + 1] = grade[128:256]
        if j == 0:
            share(cot, cot_moves, True)
    arrive(ring[0] + ring[1])
    share(cot, cot_moves, False)
    settle(cot_moves)

    def units_of(px):
        dact = lax.dot_general(rows_of(w_o[:, :, px]), cot[...], last, preferred_element_type=F32)
        value = (dact * slope[px]).astype(BF16)
        dpre[px] = value
        return jnp.dot(value, tok[:, 0:CX], preferred_element_type=F32).reshape(NZ, NL, OWN, CX)

    x_moves = []
    for k, p in enumerate(near_x):
        g_s[k] = units_of((x + p["dx"] + NX) % NX).astype(BF16)
        x_moves.append(send(g_s.at[k], g_r.at[k], peer(**p)))
    total = units_of(x)
    rest = jnp.dot(dpre[...].reshape(UNITS, ROWS), tok[:, CX:D], preferred_element_type=F32)
    for px in range(NX):
        h_s[:, px] = rest[px * 128 : (px + 1) * 128].reshape(NZ, NL, OWN, D - CX).astype(BF16)
    far_z = near_z[::-1]
    z_moves = [send(h_s.at[(z + p["dz"] + NZ) % NZ], h_r.at[k], peer(**p)) for k, p in enumerate(far_z)]

    pair = []
    for k, dy in enumerate((2, 1, -1, 0)):
        span = pl.ds(pl.multiple_of(((yh + dy + NY) % NY) * 256, 256), 256)
        weights = jnp.concatenate([rows_of(w_o[:, :, px, :, span]) for px in range(NX)], axis=0)
        term = jnp.dot(act[...], weights, preferred_element_type=F32)
        mix_s[k] = term.astype(BF16)
        theirs = pl.ds(pl.multiple_of((1 - c) * 128, 128), 128)
        pair.append(send(mix_s.at[k, :, theirs], mix_r.at[k], peer(**sibling)))
    mine = pl.ds(pl.multiple_of(c * 128, 128), 128)
    out_moves = []
    for k, p in enumerate(near_y):
        pair[k].wait_recv()
        mix_o[k] = (mix_s[k, :, mine].astype(F32) + mix_r[k].astype(F32)).astype(BF16)
        out_moves.append(send(mix_o.at[k], mix_in.at[k], peer(**p)))

    arrive(x_moves)
    total = total + (g_r[0].astype(F32) + g_r[1].astype(F32) + g_r[2].astype(F32))
    g_p[...] = total.astype(BF16)
    lz_moves = []
    for k, p in enumerate(near_lz):
        block = g_p.at[(z + p["dz"] + NZ) % NZ, (yl + p["dl"]) % NL]
        lz_moves.append(send(block, g_q.at[k], peer(**p)))

    side = h_s[z].astype(F32)
    for k, copy in enumerate(z_moves):
        copy.wait_recv()
        side = side + h_r[k].astype(F32)
    h_p[...] = side.astype(BF16)
    xl_moves = []
    for k, p in enumerate(near_xl):
        block = h_p.at[(x + p["dx"] + NX) % NX, (yl + p["dl"]) % NL]
        xl_moves.append(send(block, h_q.at[k], peer(**p)))

    pair[3].wait_recv()
    result = mix_s[3, :, mine].astype(F32) + mix_r[3].astype(F32)
    for k in range(3):
        out_moves[k].wait_recv()
        result = result + mix_in[k].astype(F32)
    mixed_out[...] = result.astype(BF16)

    scale = 1.0 / math.sqrt(ROWS * NX * NL * NZ)
    total = h_p[x, yl].astype(F32)
    for k in range(len(near_xl)):
        xl_moves[k].wait_recv()
        total = total + h_q[k].astype(F32)
    grad_out[:, CX:D] = total * scale
    total = g_p[z, yl].astype(F32)
    for k in range(len(near_lz)):
        lz_moves[k].wait_recv()
        total = total + g_q[k].astype(F32)
    grad_out[:, 0:CX] = total * scale

    for copy in started:
        copy.wait_send()


def on_device(tokens, cotangent, w_in, b_in, w_out):
    vmem = pl.BlockSpec(memory_space=pltpu.VMEM)
    return pl.pallas_call(
        kernel,
        out_shape=(
            jax.ShapeDtypeStruct((ROWS, 128), BF16),
            jax.ShapeDtypeStruct((OWN, D), F32),
        ),
        in_specs=[pl.BlockSpec(memory_space=pltpu.HBM)] * 5,
        out_specs=(vmem, vmem),
        scratch_shapes=[
            pltpu.VMEM((ROWS, D), BF16),
            pltpu.VMEM((ROWS, D), BF16),
            pltpu.VMEM((NX, NZ, NL, OWN, BW), BF16),
            pltpu.VMEM((NZ, NL, NX, OWN, D), BF16),
            pltpu.VMEM((1, OWN), BF16),
            pltpu.VMEM((ROWS, UNITS), BF16),
            pltpu.VMEM((NX, UNITS // NX, ROWS), F32),
            pltpu.VMEM((NX, UNITS // NX, ROWS), BF16),
            pltpu.VMEM((4, ROWS, 256), BF16),
            pltpu.VMEM((4, ROWS, 128), BF16),
            pltpu.VMEM((3, ROWS, 128), BF16),
            pltpu.VMEM((3, ROWS, 128), BF16),
            pltpu.VMEM((3, NZ, NL, OWN, CX), BF16),
            pltpu.VMEM((3, NZ, NL, OWN, CX), BF16),
            pltpu.VMEM((NZ, NL, OWN, CX), BF16),
            pltpu.VMEM((NL * NZ - 1, OWN, CX), BF16),
            pltpu.VMEM((NZ, NX, NL, OWN, D - CX), BF16),
            pltpu.VMEM((NZ - 1, NX, NL, OWN, D - CX), BF16),
            pltpu.VMEM((NX, NL, OWN, D - CX), BF16),
            pltpu.VMEM((NX * NL - 1, OWN, D - CX), BF16),
            pltpu.SemaphoreType.DMA((150,)),
            pltpu.SemaphoreType.DMA((150,)),
            pltpu.SemaphoreType.DMA((5,)),
        ],
        compiler_params=pltpu.CompilerParams(
            collective_id=0, has_side_effects=True, vmem_limit_bytes=60 * 1024 * 1024
        ),
        cost_estimate=pl.CostEstimate(flops=2147483648, bytes_accessed=8388608, transcendentals=262144),
    )(tokens, cotangent, w_in, b_in.reshape(1, OWN), w_out)


def solution(mesh):
    in_specs = (
        P("dp", "tensor"),
        P("dp", "tensor"),
        P(("dp", "tensor"), None),
        P(("dp", "tensor")),
        P(("dp", "tensor"), None),
    )
    out_specs = (P("dp", "tensor"), P(("dp", "tensor"), None))
    return jax.shard_map(
        on_device, mesh=mesh, in_specs=in_specs, out_specs=out_specs, check_vma=False
    )
```

time: 83.6 us -> 72.2 us (0.86)
  Pallas kernels: 77.5 us -> 69.2 us
  local copies, waits for them, and re-layouts: 5.16 us -> 2.19 us
    pallas_call x1, Pallas kernels: 77.5 us -> 69.2 us  [on_device(): pl.pallas_call(kernel, out_shape=(jax.ShapeDtypeStruct((ROWS, 128), BF16)...]
    unnamed x12 -> x4, local copies, waits for them, and re-layouts: 5.16 us -> 2.19 us
where the time goes in v2:
time: 72.2 us; the launch traced here: 72 us
  Pallas kernels  69.2 us (96%)
  local copies, waits for them, and re-layouts  2.19 us (3%)
    pallas_call x1, Pallas kernels, on_device(): pl.pallas_call(kernel, out_shape=(jax.ShapeDtypeStruct((ROWS, 128), BF16)...  69.2 us
    unnamed x4, local copies, waits for them, and re-layouts  2.19 us

profile of v2, /device:TPU:1, one launch (start us, length us, event | category | flops | bytes accessed | tf_op | source)
XLA Modules:
  0.0 72.0 jit_solution(5835098364984343998)
XLA Ops:
  0.6 69.2 %shard_map.68 = (bf16[512,128]{1,0:T(8,128)(2,1)}, f32[8,1024]{1,0:T(8,128)}) custom-call(bf16[512,128]{1,0:T(8,128)(2,1)} %tok_in.1, bf16[512,128]{1,0:T(8,128)(2,1)} %cot_in.1, bf16[8,1024]{1,0:T(8,128)(2,1)} %win_in.1, bf16[1,8]{1,0:T(2,128)(2,1)} %bitcast.1, bf16[8,1024]{1,0:T(8,128)(2,1)} %wout_in.1), custom_call_target="tpu_custom_call" | custom-call | flops 2147483648 | bytes 8388608 | tf_op jit(solution)/shard_map/pallas_call | solution.py:287
  69.8 0.0 copy-start
  69.8 1.6 %copy.9 = bf16[512,128]{1,0:T(8,128)(2,1)} copy(bf16[512,128]{1,0:T(8,128)(2,1)} %get-tuple-element.4) | data formatting | bytes 262144
  71.4 0.0 copy-done
  71.4 0.6 copy.10
Async XLA Ops:
  69.8 1.6 %copy-start = (f32[8,1024]{1,0:T(8,128)S(1)}, f32[8,1024]{1,0:T(8,128)}, u32[]{:S(2)}) copy-start(f32[8,1024]{1,0:T(8,128)} %get-tuple-element.5) | copy-start | bytes 98308

commit v3 on v2

--- a/solution.py
+++ b/solution.py
@@ -103,7 +103,7 @@
         out["dn_b"] = send(place(buf, bottom, 0), place(buf, bottom, 0), peer(dy=-1))
         out["up_b"] = send(place(buf, bottom, 0), place(buf, bottom, 0), peer(dy=1))
         out["dn_a"] = send(place(buf, top, 0), place(buf, top, 0), peer(dy=-1))
-        out["sib"] = [send(place(buf, whole, 0), place(buf, whole, 0), peer(**sibling))]
+        out["sib"] = []
         return out
 
     def pass_on(buf, out):
@@ -151,11 +151,11 @@
                 out.append(send(w_o.at[pz, l], w_o.at[pz, l], peer(dz=sign)))
         return out
 
-    tok_moves = spread(tok)
     wi_own = send(w_i.at[x, z, yl], w_i.at[x, z, yl], peer(**partner))
     wo_own = send(w_o.at[z, yl, x], w_o.at[z, yl, x], peer(**partner))
     wo_moves = wo_to_x(yl)
     wi_moves = wi_to_z(yl)
+    tok_moves = spread(tok)
     wi_own.wait_recv()
     wi_more = wi_to_z(1 - yl)
     wi_second = wi_to_x(0)
@@ -172,20 +172,27 @@
         return out
 
     arrive(wo_moves)
-    ring = [ring_step(1, 0)]
+    ring = [ring_step(1, 0), None]
     wi_second += relay(1, -1)
+    cot_moves = spread(cot)
+    for buf, moves in ((tok, tok_moves), (cot, cot_moves)):
+        moves['sib'].append(send(place(buf, whole, 0), place(buf, whole, 0), peer(**sibling)))
     arrive(wo_more)
-    ring.append(ring_step(1, 1))
+    ring[1] = ring_step(1, 1)
+    wi_second += relay(2, -2)
+    ring[0] = ring_step(2, 0, ring[0])
+    wi_second += relay(3, -3)
+    wi_second += relay(4)
+    ring[1] = ring_step(2, 1, ring[1])
     pass_on(tok, tok_moves)
-    cot_moves = spread(cot)
-    wi_second += relay(2, -2)
-    ring = [ring_step(2, h, ring[h]) for h in (0, 1)]
-    wi_second += relay(3, -3, 4)
+    ring[0] = ring_step(3, 0, ring[0])
+    ring[1] = ring_step(3, 1, ring[1])
+    pass_on(cot, cot_moves)
+    ring[0] = ring_step(4, 0, ring[0])
+    ring[1] = ring_step(4, 1, ring[1])
     share(tok, tok_moves, True)
-    ring = [ring_step(3, h, ring[h]) for h in (0, 1)]
     share(tok, tok_moves, False)
-    pass_on(cot, cot_moves)
-    ring = [ring_step(4, h, ring[h]) for h in (0, 1)]
+    share(cot, cot_moves, True)
     arrive(wi_second)
     settle(tok_moves)
 
@@ -203,10 +210,22 @@
         act[:, j * 256 : (j + 1) * 256] = value.astype(BF16).T
         slope[2 * j] = grade[0:128]
         slope[2 * j + 1] = grade[128:256]
-        if j == 0:
-            share(cot, cot_moves, True)
     arrive(ring[0] + ring[1])
+    pair = []
+    for k, dy in enumerate((2, 1, -1, 0)):
+        span = pl.ds(pl.multiple_of(((yh + dy + NY) % NY) * 256, 256), 256)
+        weights = jnp.concatenate([rows_of(w_o[:, :, px, :, span]) for px in range(NX)], axis=0)
+        term = jnp.dot(act[...], weights, preferred_element_type=F32)
+        mix_s[k] = term.astype(BF16)
+        theirs = pl.ds(pl.multiple_of((1 - c) * 128, 128), 128)
+        pair.append(send(mix_s.at[k, :, theirs], mix_r.at[k], peer(**sibling)))
     share(cot, cot_moves, False)
+    mine = pl.ds(pl.multiple_of(c * 128, 128), 128)
+    out_moves = []
+    for k, p in enumerate(near_y):
+        pair[k].wait_recv()
+        mix_o[k] = (mix_s[k, :, mine].astype(F32) + mix_r[k].astype(F32)).astype(BF16)
+        out_moves.append(send(mix_o.at[k], mix_in.at[k], peer(**p)))
     settle(cot_moves)
 
     def units_of(px):
@@ -226,20 +245,6 @@
     far_z = near_z[::-1]
     z_moves = [send(h_s.at[(z + p["dz"] + NZ) % NZ], h_r.at[k], peer(**p)) for k, p in enumerate(far_z)]
 
-    pair = []
-    for k, dy in enumerate((2, 1, -1, 0)):
-        span = pl.ds(pl.multiple_of(((yh + dy + NY) % NY) * 256, 256), 256)
-        weights = jnp.concatenate([rows_of(w_o[:, :, px, :, span]) for px in range(NX)], axis=0)
-        term = jnp.dot(act[...], weights, preferred_element_type=F32)
-        mix_s[k] = term.astype(BF16)
-        theirs = pl.ds(pl.multiple_of((1 - c) * 128, 128), 128)
-        pair.append(send(mix_s.at[k, :, theirs], mix_r.at[k], peer(**sibling)))
-    mine = pl.ds(pl.multiple_of(c * 128, 128), 128)
-    out_moves = []
-    for k, p in enumerate(near_y):
-        pair[k].wait_recv()
-        mix_o[k] = (mix_s[k, :, mine].astype(F32) + mix_r[k].astype(F32)).astype(BF16)
-        out_moves.append(send(mix_o.at[k], mix_in.at[k], peer(**p)))
 
     arrive(x_moves)
     total = total + (g_r[0].astype(F32) + g_r[1].astype(F32) + g_r[2].astype(F32))

time: 72.2 us -> 67.9 us (0.940)
  Pallas kernels: 69.2 us -> 64.9 us
    pallas_call x1, Pallas kernels: 69.2 us -> 64.9 us  [on_device(): pl.pallas_call(kernel, out_shape=(jax.ShapeDtypeStruct((ROWS, 128), BF16)...]
where the time goes in v3:
time: 67.9 us; the launch traced here: 67.7 us
  Pallas kernels  64.9 us (96%)
  local copies, waits for them, and re-layouts  2.19 us (3%)
    pallas_call x1, Pallas kernels, on_device(): pl.pallas_call(kernel, out_shape=(jax.ShapeDtypeStruct((ROWS, 128), BF16)...  64.9 us
    unnamed x4, local copies, waits for them, and re-layouts  2.19 us

profile of v3, /device:TPU:1, one launch (start us, length us, event | category | flops | bytes accessed | tf_op | source)
XLA Modules:
  0.0 67.7 jit_solution(13209107103816846800)
XLA Ops:
  0.6 64.9 %shard_map.68 = (bf16[512,128]{1,0:T(8,128)(2,1)}, f32[8,1024]{1,0:T(8,128)}) custom-call(bf16[512,128]{1,0:T(8,128)(2,1)} %tok_in.1, bf16[512,128]{1,0:T(8,128)(2,1)} %cot_in.1, bf16[8,1024]{1,0:T(8,128)(2,1)} %win_in.1, bf16[1,8]{1,0:T(2,128)(2,1)} %bitcast.1, bf16[8,1024]{1,0:T(8,128)(2,1)} %wout_in.1), custom_call_target="tpu_custom_call" | custom-call | flops 2147483648 | bytes 8388608 | tf_op jit(solution)/shard_map/pallas_call | solution.py:292
  65.5 0.0 copy-start
  65.6 1.6 %copy.9 = bf16[512,128]{1,0:T(8,128)(2,1)} copy(bf16[512,128]{1,0:T(8,128)(2,1)} %get-tuple-element.4) | data formatting | bytes 262144
  67.1 0.0 copy-done
  67.1 0.6 copy.10
Async XLA Ops:
  65.5 1.6 %copy-start = (f32[8,1024]{1,0:T(8,128)S(1)}, f32[8,1024]{1,0:T(8,128)}, u32[]{:S(2)}) copy-start(f32[8,1024]{1,0:T(8,128)} %get-tuple-element.5) | copy-start | bytes 98308

commit v4 on v3

--- a/solution.py
+++ b/solution.py
@@ -15,6 +15,7 @@
 BW = D + 128
 HALF = ROWS // 2
 CX = 768
+CH = CX // 2
 
 
 def gelu_parts(value):
@@ -234,11 +235,15 @@
         dpre[px] = value
         return jnp.dot(value, tok[:, 0:CX], preferred_element_type=F32).reshape(NZ, NL, OWN, CX)
 
-    x_moves = []
+    x_moves = [[], []]
     for k, p in enumerate(near_x):
-        g_s[k] = units_of((x + p["dx"] + NX) % NX).astype(BF16)
-        x_moves.append(send(g_s.at[k], g_r.at[k], peer(**p)))
-    total = units_of(x)
+        value = units_of((x + p["dx"] + NX) % NX).astype(BF16)
+        for h in range(2):
+            g_s[h, k] = value[..., h * CH : (h + 1) * CH]
+        x_moves[0].append(send(g_s.at[0, k], g_r.at[0, k], peer(**p)))
+    for k, p in enumerate(near_x):
+        x_moves[1].append(send(g_s.at[1, k], g_r.at[1, k], peer(**p)))
+    own = units_of(x)
     rest = jnp.dot(dpre[...].reshape(UNITS, ROWS), tok[:, CX:D], preferred_element_type=F32)
     for px in range(NX):
         h_s[:, px] = rest[px * 128 : (px + 1) * 128].reshape(NZ, NL, OWN, D - CX).astype(BF16)
@@ -246,14 +251,17 @@
     z_moves = [send(h_s.at[(z + p["dz"] + NZ) % NZ], h_r.at[k], peer(**p)) for k, p in enumerate(far_z)]
 
 
-    arrive(x_moves)
-    total = total + (g_r[0].astype(F32) + g_r[1].astype(F32) + g_r[2].astype(F32))
-    g_p[...] = total.astype(BF16)
-    lz_moves = []
-    for k, p in enumerate(near_lz):
-        block = g_p.at[(z + p["dz"] + NZ) % NZ, (yl + p["dl"]) % NL]
-        lz_moves.append(send(block, g_q.at[k], peer(**p)))
-
+    def over_lz(h):
+        arrive(x_moves[h])
+        total = own[..., h * CH : (h + 1) * CH] + (g_r[h, 0].astype(F32) + g_r[h, 1].astype(F32) + g_r[h, 2].astype(F32))
+        g_p[h] = total.astype(BF16)
+        moves = []
+        for k, p in enumerate(near_lz):
+            block = g_p.at[h, (z + p["dz"] + NZ) % NZ, (yl + p["dl"]) % NL]
+            moves.append(send(block, g_q.at[h, k], peer(**p)))
+        return moves
+
+    lz_moves = [over_lz(0)]
     side = h_s[z].astype(F32)
     for k, copy in enumerate(z_moves):
         copy.wait_recv()
@@ -263,6 +271,7 @@
     for k, p in enumerate(near_xl):
         block = h_p.at[(x + p["dx"] + NX) % NX, (yl + p["dl"]) % NL]
         xl_moves.append(send(block, h_q.at[k], peer(**p)))
+    lz_moves.append(over_lz(1))
 
     pair[3].wait_recv()
     result = mix_s[3, :, mine].astype(F32) + mix_r[3].astype(F32)
@@ -277,11 +286,12 @@
         xl_moves[k].wait_recv()
         total = total + h_q[k].astype(F32)
     grad_out[:, CX:D] = total * scale
-    total = g_p[z, yl].astype(F32)
-    for k in range(len(near_lz)):
-        lz_moves[k].wait_recv()
-        total = total + g_q[k].astype(F32)
-    grad_out[:, 0:CX] = total * scale
+    for h in range(2):
+        total = g_p[h, z, yl].astype(F32)
+        for k in range(len(near_lz)):
+            lz_moves[h][k].wait_recv()
+            total = total + g_q[h, k].astype(F32)
+        grad_out[:, h * CH : (h + 1) * CH] = total * scale
 
     for copy in started:
         copy.wait_send()
@@ -310,16 +320,16 @@
             pltpu.VMEM((4, ROWS, 128), BF16),
             pltpu.VMEM((3, ROWS, 128), BF16),
             pltpu.VMEM((3, ROWS, 128), BF16),
-            pltpu.VMEM((3, NZ, NL, OWN, CX), BF16),
-            pltpu.VMEM((3, NZ, NL, OWN, CX), BF16),
-            pltpu.VMEM((NZ, NL, OWN, CX), BF16),
-            pltpu.VMEM((NL * NZ - 1, OWN, CX), BF16),
+            pltpu.VMEM((2, 3, NZ, NL, OWN, CH), BF16),
+            pltpu.VMEM((2, 3, NZ, NL, OWN, CH), BF16),
+            pltpu.VMEM((2, NZ, NL, OWN, CH), BF16),
+            pltpu.VMEM((2, NL * NZ - 1, OWN, CH), BF16),
             pltpu.VMEM((NZ, NX, NL, OWN, D - CX), BF16),
             pltpu.VMEM((NZ - 1, NX, NL, OWN, D - CX), BF16),
             pltpu.VMEM((NX, NL, OWN, D - CX), BF16),
             pltpu.VMEM((NX * NL - 1, OWN, D - CX), BF16),
-            pltpu.SemaphoreType.DMA((150,)),
-            pltpu.SemaphoreType.DMA((150,)),
+            pltpu.SemaphoreType.DMA((170,)),
+            pltpu.SemaphoreType.DMA((170,)),
             pltpu.SemaphoreType.DMA((5,)),
         ],
         compiler_params=pltpu.CompilerParams(

time: 67.9 us -> 67.2 us (0.990)
  Pallas kernels: 64.9 us -> 64.2 us
    pallas_call x1, Pallas kernels: 64.9 us -> 64.2 us  [on_device(): pl.pallas_call(kernel, out_shape=(jax.ShapeDtypeStruct((ROWS, 128), BF16)...]
where the time goes in v4:
time: 67.2 us; the launch traced here: 67 us
  Pallas kernels  64.2 us (96%)
  local copies, waits for them, and re-layouts  2.19 us (3%)
    pallas_call x1, Pallas kernels, on_device(): pl.pallas_call(kernel, out_shape=(jax.ShapeDtypeStruct((ROWS, 128), BF16)...  64.2 us
    unnamed x4, local copies, waits for them, and re-layouts  2.19 us

profile of v4, /device:TPU:1, one launch (start us, length us, event | category | flops | bytes accessed | tf_op | source)
XLA Modules:
  0.0 67.0 jit_solution(11514680927677640346)
XLA Ops:
  0.6 64.2 %shard_map.68 = (bf16[512,128]{1,0:T(8,128)(2,1)}, f32[8,1024]{1,0:T(8,128)}) custom-call(bf16[512,128]{1,0:T(8,128)(2,1)} %tok_in.1, bf16[512,128]{1,0:T(8,128)(2,1)} %cot_in.1, bf16[8,1024]{1,0:T(8,128)(2,1)} %win_in.1, bf16[1,8]{1,0:T(2,128)(2,1)} %bitcast.1, bf16[8,1024]{1,0:T(8,128)(2,1)} %wout_in.1), custom_call_target="tpu_custom_call" | custom-call | flops 2147483648 | bytes 8388608 | tf_op jit(solution)/shard_map/pallas_call | solution.py:302
  64.8 0.0 copy-start
  64.8 1.6 %copy.9 = bf16[512,128]{1,0:T(8,128)(2,1)} copy(bf16[512,128]{1,0:T(8,128)(2,1)} %get-tuple-element.4) | data formatting | bytes 262144
  66.4 0.0 copy-done
  66.4 0.6 copy.10
Async XLA Ops:
  64.8 1.6 %copy-start = (f32[8,1024]{1,0:T(8,128)S(1)}, f32[8,1024]{1,0:T(8,128)}, u32[]{:S(2)}) copy-start(f32[8,1024]{1,0:T(8,128)} %get-tuple-element.5) | copy-start | bytes 98308

commit v5 on v4

--- a/solution.py
+++ b/solution.py
@@ -134,9 +134,9 @@
     def wi_to_z(l):
         return [send(w_i.at[x, z, l], w_i.at[x, z, l], peer(**p)) for p in near_z]
 
-    def wi_to_x(dz):
-        pz = (z + dz + NZ) % NZ
-        return [send(w_i.at[x, pz], w_i.at[x, pz], peer(**p)) for p in near_x]
+    def wi_to_x(dz, l):
+        block = w_i.at[x, (z + dz + NZ) % NZ, l]
+        return [send(block, block, peer(**p)) for p in near_x]
 
     def wo_to_x(l):
         return [send(w_o.at[z, l, x], w_o.at[z, l, x], peer(**p)) for p in near_x]
@@ -155,43 +155,46 @@
     wi_own = send(w_i.at[x, z, yl], w_i.at[x, z, yl], peer(**partner))
     wo_own = send(w_o.at[z, yl, x], w_o.at[z, yl, x], peer(**partner))
     wo_moves = wo_to_x(yl)
+    wi_second = wi_to_x(0, yl)
     wi_moves = wi_to_z(yl)
     tok_moves = spread(tok)
     wi_own.wait_recv()
+    wi_second += wi_to_x(0, 1 - yl)
     wi_more = wi_to_z(1 - yl)
-    wi_second = wi_to_x(0)
     wo_own.wait_recv()
     wo_more = wo_to_x(1 - yl)
 
-    def relay(*dzs):
+    def relay(moves, l, *dzs):
         out = []
         for dz in dzs:
-            k = [p["dz"] for p in near_z].index(-dz if dz != 4 else 4)
-            wi_moves[k].wait_recv()
-            wi_more[k].wait_recv()
-            out += wi_to_x(dz)
+            moves[[p["dz"] for p in near_z].index(-dz if dz != 4 else 4)].wait_recv()
+            out += wi_to_x(dz, l)
         return out
 
     arrive(wo_moves)
     ring = [ring_step(1, 0), None]
-    wi_second += relay(1, -1)
+    wi_second += relay(wi_moves, yl, 1, -1)
+    arrive(wo_more)
+    ring[1] = ring_step(1, 1)
+    wi_second += relay(wi_moves, yl, 2, -2)
     cot_moves = spread(cot)
     for buf, moves in ((tok, tok_moves), (cot, cot_moves)):
-        moves['sib'].append(send(place(buf, whole, 0), place(buf, whole, 0), peer(**sibling)))
-    arrive(wo_more)
-    ring[1] = ring_step(1, 1)
-    wi_second += relay(2, -2)
+        moves["sib"].append(send(place(buf, whole, 0), place(buf, whole, 0), peer(**sibling)))
     ring[0] = ring_step(2, 0, ring[0])
-    wi_second += relay(3, -3)
-    wi_second += relay(4)
+    wi_second += relay(wi_moves, yl, 3, -3)
+    wi_second += relay(wi_moves, yl, 4)
     ring[1] = ring_step(2, 1, ring[1])
+    wi_second += relay(wi_more, 1 - yl, 1, -1)
+    wi_second += relay(wi_more, 1 - yl, 2, -2)
     pass_on(tok, tok_moves)
     ring[0] = ring_step(3, 0, ring[0])
+    wi_second += relay(wi_more, 1 - yl, 3, -3)
+    wi_second += relay(wi_more, 1 - yl, 4)
     ring[1] = ring_step(3, 1, ring[1])
+    share(tok, tok_moves, True)
     pass_on(cot, cot_moves)
     ring[0] = ring_step(4, 0, ring[0])
     ring[1] = ring_step(4, 1, ring[1])
-    share(tok, tok_moves, True)
     share(tok, tok_moves, False)
     share(cot, cot_moves, True)
     arrive(wi_second)
@@ -328,8 +331,8 @@
             pltpu.VMEM((NZ - 1, NX, NL, OWN, D - CX), BF16),
             pltpu.VMEM((NX, NL, OWN, D - CX), BF16),
             pltpu.VMEM((NX * NL - 1, OWN, D - CX), BF16),
-            pltpu.SemaphoreType.DMA((170,)),
-            pltpu.SemaphoreType.DMA((170,)),
+            pltpu.SemaphoreType.DMA((200,)),
+            pltpu.SemaphoreType.DMA((200,)),
             pltpu.SemaphoreType.DMA((5,)),
         ],
         compiler_params=pltpu.CompilerParams(

time: 67.2 us -> 66.9 us (level)
  no operation moved by 1% of the time
where the time goes in v5:
time: 66.9 us; the launch traced here: 66.8 us
  Pallas kernels  63.9 us (96%)
  local copies, waits for them, and re-layouts  2.19 us (3%)
    pallas_call x1, Pallas kernels, on_device(): pl.pallas_call(kernel, out_shape=(jax.ShapeDtypeStruct((ROWS, 128), BF16)...  63.9 us
    unnamed x4, local copies, waits for them, and re-layouts  2.19 us

profile of v5, /device:TPU:1, one launch (start us, length us, event | category | flops | bytes accessed | tf_op | source)
XLA Modules:
  0.0 66.8 jit_solution(11482496301132599937)
XLA Ops:
  0.6 63.9 %shard_map.68 = (bf16[512,128]{1,0:T(8,128)(2,1)}, f32[8,1024]{1,0:T(8,128)}) custom-call(bf16[512,128]{1,0:T(8,128)(2,1)} %tok_in.1, bf16[512,128]{1,0:T(8,128)(2,1)} %cot_in.1, bf16[8,1024]{1,0:T(8,128)(2,1)} %win_in.1, bf16[1,8]{1,0:T(2,128)(2,1)} %bitcast.1, bf16[8,1024]{1,0:T(8,128)(2,1)} %wout_in.1), custom_call_target="tpu_custom_call" | custom-call | flops 2147483648 | bytes 8388608 | tf_op jit(solution)/shard_map/pallas_call | solution.py:305
  64.6 0.0 copy-start
  64.6 1.6 %copy.9 = bf16[512,128]{1,0:T(8,128)(2,1)} copy(bf16[512,128]{1,0:T(8,128)(2,1)} %get-tuple-element.4) | data formatting | bytes 262144
  66.2 0.0 copy-done
  66.2 0.6 copy.10
Async XLA Ops:
  64.6 1.6 %copy-start = (f32[8,1024]{1,0:T(8,128)S(1)}, f32[8,1024]{1,0:T(8,128)}, u32[]{:S(2)}) copy-start(f32[8,1024]{1,0:T(8,128)} %get-tuple-element.5) | copy-start | bytes 98308
